TPU v7x, 256 devices: a whole 4x4x8 slice. The times are simulated.
256 devices in a mesh: query: 8 (over x, y_hi), lib: 32 (over z, y_lo, core).
Axes of the slice: x: 4, y: 4 (y_hi: 2, y_lo: 2; y = y_hi * 2 + y_lo), z: 8, core: 2. Of those that a mesh axis runs over, the one named last changes fastest.
Arguments:
- query_words: int32 [1024, 64], P(('query', 'lib')), may hold values from -2147483648 to 2147483647, as said below
- lib_bits: bfloat16 [262144, 2048], P('lib'), may hold values from 0 to 1, as said below
- cutoff: float32 [262144], P('lib'), may hold values from 0.05 to 0.35
- counts: int32 [512], P('lib'), may hold values from 1 to 8, as said below
- targets: int32 [512, 8], P('lib'), may hold values from 0 to 63
- activity_tiles: bfloat16 [512, 8, 512, 128], P('lib'), may hold values from 0 to 1
Outputs:
- centered_scores: float32 [8192, 1024], P('lib', 'query')
Inputs may be any that keep to these rules, and one draw needn't show every extreme that they name: `query_words`: bit k of word w (bit 31 the sign bit, two's complement) is fingerprint bit 32 w + k; some queries have no bit set. `lib_bits`: entries are 0 or 1; some library compounds have no bit set. `counts`: some library block has all 8 slots live.
All inputs are finite; a program needn't handle non-finite values.
Results may differ from a plain program's by a relative error of at most 0.0003.
Values sent between devices are 32-bit elements; how exact they have to be, the bound alone decides.
A program may use at most 192 MiB of HBM per device.

v0:
```python
import jax
import jax.numpy as jnp
from jax import lax
from jax.sharding import PartitionSpec as P

NT = 8192
TBLK = 128
BLOCK = 512
KMAX = 8


alpha_weight = 0.7
beta_weight = 0.3
steepness = 16.0


def unpack(words):
    shifts = jnp.arange(32, dtype=jnp.int32)
    bit_table = jnp.right_shift(words[:, :, None], shifts[None, None, :]) & 1
    return bit_table.reshape(words.shape[0], words.shape[1] * 32).astype(jnp.bfloat16)


def screen(words, lib_bits, library_count, cutoff):
    query_bits = unpack(words)
    query_count = jnp.sum(query_bits, axis=1, dtype=jnp.float32)
    intersection = lax.dot_general(
        lib_bits, query_bits, (((1,), (1,)), ((), ())), preferred_element_type=jnp.float32
    )
    denominator = jnp.maximum(
        alpha_weight * query_count[None, :] + beta_weight * library_count[:, None], 1.0
    )
    similarity = intersection / denominator
    return jax.nn.sigmoid(steepness * (similarity - cutoff[:, None])).astype(jnp.bfloat16)


def local(query_words, lib_bits, cutoff, counts, targets, activity_tiles):
    group_queries = query_words.shape[0] * lax.axis_size("lib")
    library_count = jnp.sum(lib_bits, axis=1, dtype=jnp.float32)
    panel_words = lax.all_gather(query_words, "lib", axis=0, tiled=True)
    soft_hits = screen(panel_words, lib_bits, library_count, cutoff)
    block_total = counts.shape[0]
    slot_total = block_total * KMAX
    block_hits = soft_hits.reshape(block_total, BLOCK, group_queries)
    slot_terms = jnp.einsum(
        "bkiu,biq->bkuq", activity_tiles, block_hits, preferred_element_type=jnp.float32
    )
    slot_terms = slot_terms.reshape(slot_total, TBLK * group_queries)
    slot_index = jnp.arange(KMAX, dtype=jnp.int32)
    live_weight = jnp.where(slot_index[None, :] < counts[:, None], 1.0 / BLOCK, 0.0).astype(
        jnp.float32
    )
    live_weight = live_weight.reshape(slot_total)
    slot_target = targets.reshape(slot_total)
    block_count = NT // TBLK
    first_block = 0 // TBLK
    wanted = first_block + jnp.arange(block_count, dtype=jnp.int32)
    routing = jnp.where(wanted[:, None] == slot_target[None, :], live_weight[None, :], 0.0)
    totals = jnp.dot(
        routing, slot_terms, precision=lax.Precision.HIGHEST, preferred_element_type=jnp.float32
    )
    partial_scores = totals.reshape(NT, group_queries)
    raw_scores = lax.psum_scatter(partial_scores, "lib", scatter_dimension=0, tiled=True)
    colsum = jnp.sum(raw_scores, axis=1)
    target_total = lax.psum(colsum, "query")
    target_mean = target_total / (group_queries * lax.axis_size("query"))
    return raw_scores - target_mean[:, None]


def solution(mesh):
    in_specs = (
        P(("query", "lib"), None),
        P("lib", None),
        P("lib"),
        P("lib"),
        P("lib", None),
        P("lib", None, None, None),
    )
    out_specs = P("lib", "query")
    return jax.shard_map(local, mesh=mesh, in_specs=in_specs, out_specs=out_specs, check_vma=False)
```

profile of v0, /device:TPU:1, one launch (start us, length us, event | category | flops | bytes accessed | tf_op | source)
XLA Modules:
  0.0 264.4 jit_solution(6859467453568927737)
XLA Ops:
  6.5 0.0 reduce-scatter.2.cloned.1.call-start
  6.5 38.9 %all-gather = s32[32,4,64]{2,1,0:T(4,128)S(1)} all-gather(s32[1,4,64]{2,1,0:T(4,128)} %bitcast.45), channel_id=1, replica_groups=mesh['query'=8,'lib'=32] {'lib'}, dimensions={0}, use_global_device_ids=true | all-gather | bytes 33792 | tf_op jit(solution)/shard_map/all_gather | solution.py:39
  45.5 0.1 copy.14
  45.6 0.1 shift_right_arithmetic.28
  45.6 0.3 convert_reduce_fusion.1
  45.9 0.3 fusion.13
  46.3 0.0 copy-start.2
  46.3 11.2 %convert_reduce_fusion = f32[8192]{0:T(1024)S(1)} fusion(bf16[8192,2048]{1,0:T(8,128)(2,1)} %param.7), kind=kLoop, calls=%fused_computation | loop fusion | flops 33546240 | bytes 33587200 | tf_op jit(solution)/shard_map/reduce_sum | solution.py:38
  57.5 17.2 %fusion.7 = bf16[8192,128]{0,1:T(8,128)(2,1)S(1)} fusion(bf16[128,2048]{0,1:T(8,128)(2,1)S(1)} %fusion.13, bf16[8192,2048]{1,0:T(8,128)(2,1)} %param.7, f32[8192]{0:T(1024)S(1)} %copy-done.2, f32[8192]{0:T(1024)S(1)} %broadcast_multiply_fusion, f32[128]{0:T(128)S(1)} %broadcast_multiply_fusion.2), kind=kOutput, calls=%fused_computation.9 | convolution fusion | flops 4304404480 | bytes 36241920 | tf_op jit(solution)/shard_map/dot_general | solution.py:26
  74.8 0.8 copy.20
  75.6 13.4 %convolution_bitcast_fusion.1 = f32[16,8,128,128]{2,3,1,0:T(8,128)} fusion(bf16[16,8,512,128]{3,2,1,0:T(8,128)(2,1)} %param.11, bf16[16,512,128,1]{1,0,2,3:T(8,128)(2,1)S(1)} %bitcast.42), kind=kOutput, calls=%fused_computation.13 | convolution fusion | flops 2147483648 | bytes 27262976 | tf_op jit(solution)/shard_map/bkiu,biq->bkuq/dot_general | solution.py:44
  89.0 9.3 %copy.16 = f32[16,8,128,128]{3,2,1,0:T(8,128)} copy(f32[16,8,128,128]{2,3,1,0:T(8,128)} %convolution_bitcast_fusion.1) | data formatting | bytes 16777216 | tf_op jit(solution)/shard_map/bkiu,biq->bkuq/dot_general | solution.py:44
  98.3 0.0 copy-done
  98.3 0.1 copy.13
  98.4 0.1 eq.16
  98.5 0.1 fusion.18
  98.5 0.1 select_n.16
  98.6 14.6 %fusion.8 = f32[64,16384]{1,0:T(8,128)} fusion(f32[16,8,128,128]{3,2,1,0:T(8,128)} %copy.16, f32[128]{0:T(128)S(1)} %select_n.16, s32[128]{0:T(128)S(1)} %eq.16), kind=kOutput, calls=%fused_computation.10 | convolution fusion | flops 1610629120 | bytes 12583936 | tf_op jit(solution)/shard_map/dot_general | solution.py:58
  113.2 4.9 %reshape.50 = f32[8192,128]{1,0:T(8,128)} reshape(f32[64,16384]{1,0:T(8,128)} %fusion.8) | data formatting | bytes 8388608 | tf_op jit(solution)/shard_map/reshape | solution.py:61
  118.1 0.0 reduce-scatter.2.cloned.1.call-update
  118.1 116.5 %reduce-scatter.2.cloned.1.call-done = f32[256,128]{1,0:T(8,128)} async-done(((f32[8192,128]{1,0:T(8,128)}), f32[256,128]{1,0:T(8,128)}) %reduce-scatter.2.cloned.1.call-update) | async-done | bytes 131088 | tf_op jit(solution)/shard_map/reduce_scatter | solution.py:62
  234.7 1.0 reduce_sum.29
  235.7 20.2 %psum.7 = f32[256]{0:T(256)S(1)} all-reduce(f32[256]{0:T(256)S(1)} %reduce_sum.29), channel_id=1, replica_groups=mesh['query'=8,'lib'=32] {'query'}, use_global_device_ids=true, to_apply=%region_4.5 | all-reduce | flops 256 | bytes 2048 | tf_op jit(solution)/shard_map/psum | solution.py:64
  255.9 1.7 broadcast_subtract_fusion
  (8 shorter events, 0.0 us)
Async XLA Ops:
  6.5 228.1 %reduce-scatter.2.cloned.1.call-start = ((), (), s32[]{:S(2)}) async-start(), calls=%async_computation.1 | async-start | bytes 4325376 | tf_op jit(solution)/shard_map/reduce_scatter | solution.py:62
  46.3 11.2 %copy-start.2 = (f32[8192]{0:T(1024)S(1)}, f32[8192]{0:T(1024)}, u32[]{:S(2)}) copy-start(f32[8192]{0:T(1024)} %param.8) | copy-start | bytes 98308
  89.0 9.3 %copy-start = (s32[16,8]{0,1:T(8,128)S(1)}, s32[16,8]{0,1:T(8,128)}, u32[]{:S(2)}) copy-start(s32[16,8]{0,1:T(8,128)} %param.10) | copy-start | bytes 1540
  89.0 9.5 %copy-start.1 = (s32[16]{0:T(128)S(1)}, s32[16]{0:T(128)}, u32[]{:S(2)}) copy-start(s32[16]{0:T(128)} %param.9) | copy-start | bytes 196
Sparse Core Ops, SparseCore 0:
  118.2 116.3 reduce-scatter.1
where the time goes:
time: 270 us; the launch traced here: 264 us
  waiting for transfers between devices  117 us (43%)
  blocking collectives  59.1 us (22%)
  matrix products  45.2 us (17%)
  local copies, waits for them, and re-layouts  15.4 us (6%)
  other arithmetic  14.6 us (5%)
  between operations  13.5 us (5%)
    reduce_scatter x1, waiting for transfers between devices, local(): lax.psum_scatter(partial_scores, 'lib', scatter_dimension=0, tiled=True)  117 us
    all_gather x1, blocking collectives, local(): panel_words = lax.all_gather(query_words, 'lib', axis=0, tiled=True)  38.9 us
    psum x1, blocking collectives, local(): target_total = lax.psum(colsum, 'query')  20.2 us
    dot_general x1, matrix products, screen(): lax.dot_general(lib_bits, query_bits, (((1,), (1,)), ((), ())), preferred...  17.2 us
    dot_general x1, matrix products, local(): jnp.dot(routing, slot_terms, precision=lax.Precision.HIGHEST, preferred_e...  14.6 us
    dot_general x1, matrix products, local(): jnp.einsum('bkiu,biq->bkuq', activity_tiles, block_hits, preferred_elemen...  13.4 us
    reduce_sum x1, other arithmetic, local(): library_count = jnp.sum(lib_bits, axis=1, dtype=jnp.float32)  11.2 us
    dot_general x1, local copies, waits for them, and re-layouts, local(): jnp.einsum('bkiu,biq->bkuq', activity_tiles, block_hits, preferred_elemen...  9.3 us
  transfers between devices with their start and end apart: 1, of which 1 were waited for; matrix products, arithmetic and copies ran while one was open for 0% of the time, Pallas kernels for 0%

commit v1 on v0

v1 whole, which is shorter than its diff:
```python
import jax
import jax.numpy as jnp
from jax import lax
from jax.experimental import pallas as pl
from jax.experimental.pallas import tpu as pltpu
from jax.sharding import PartitionSpec as P

TBLK = 128
BLOCK = 512
KMAX = 8
NBITS = 2048
WORDS = 64
ROWS = 1024
NBUF = 4
LIB = 8192
STEPS = LIB // ROWS
SLOTS = LIB // BLOCK * KMAX
QL = 128

alpha_weight = 0.7
beta_weight = 0.3
steepness = 16.0

F8 = jnp.float8_e4m3fn
BF = jnp.bfloat16
F32 = jnp.float32
MESH = pl.DeviceIdType.MESH

ORDER = (4, 3, -3, 2, -2, 1, -1, 0)
PLACE = {d: g for g, d in enumerate(ORDER)}
RING0 = ((4, 0), (3, 1), (3, 0), (2, 1), (2, 0), (1, 1), (1, 0))


def kernel(tab, words, cut, lib, tiles, out,
           QQ, LB, TB, S, HT, C, CB, W1, WR, G, CS, CR, M0, M1, YS, YR, F0, FY,
           R0, L0, R1H, L1H, R1, L1, MS, MR, TMP,
           lsem, tsem, g1s, g1r, g2s, g2r, cs, cr, ys, yr, fs, fr,
           r0s, r0r, l0s, l0r, r1s, r1r, l1s, l1r, ms, mr):
    qi = lax.axis_index("query")
    li = lax.axis_index("lib")
    z = li // 4
    p4 = lax.rem(li, 4)
    yl = p4 // 2
    core = lax.rem(p4, 2)

    def lcp(i):
        s = lax.rem(i, NBUF)
        return pltpu.make_async_copy(
            lib.at[pl.ds(pl.multiple_of(i * ROWS, ROWS), ROWS)], LB.at[s], lsem.at[s])

    def tcp(i):
        s = lax.rem(i, NBUF)
        return pltpu.make_async_copy(
            tiles.at[pl.ds(i * (ROWS // BLOCK), ROWS // BLOCK)], TB.at[s], tsem.at[s])

    for i in range(NBUF):
        lcp(i).start()
        tcp(i).start()

    def square(k):
        return (qi, z * 4 + lax.rem(p4 + k, 4))

    def along(k):
        return (qi, lax.rem(z + k + 8, 8) * 4 + p4)

    def other(k):
        return (lax.rem(qi + k, 8), li)

    partners = [square(k) for k in (1, 2, 3)]
    partners += [along(k) for k in range(1, 8)]
    partners += [other(k) for k in range(1, 8)]
    barrier = pltpu.get_barrier_semaphore()
    for dev in partners:
        pl.semaphore_signal(barrier, inc=1, device_id=dev, device_id_type=MESH)
    pl.semaphore_wait(barrier, len(partners))

    def remote(src, dst, ssem, rsem, dev):
        return pltpu.make_async_remote_copy(
            src_ref=src, dst_ref=dst, send_sem=ssem, recv_sem=rsem,
            device_id=dev, device_id_type=MESH)

    sent = []

    def start(copy):
        copy.start()
        sent.append(copy)
        return copy

    one = [start(remote(words, WR.at[k], g1s.at[k], g1r.at[k], square(k + 1)))
           for k in range(3)]

    def cutstep(r, carry):
        for k in range(4):
            row = r * 4 + k
            CB[pl.ds(pl.multiple_of(row * 128, 128), 128), :] = jnp.broadcast_to(
                cut[pl.ds(row, 1), :], (128, 128)).T
        return carry

    for copy in one:
        copy.wait_recv()
    W1[...] = words[...] + WR[0] + WR[1] + WR[2]
    two = [start(remote(W1, G.at[z], g2s.at[k], g2r.at[k], along(k + 1)))
           for k in range(7)]
    G[z] = W1[...]
    C[SLOTS] = jnp.zeros((QL, TBLK), F32)
    QQ[:, QL:2 * QL] = jnp.ones((NBITS, QL), F32).astype(F8)
    lax.fori_loop(0, 16, cutstep, 0)
    for copy in two:
        copy.wait_recv()

    turned = G[...].reshape(64, 128).T
    panel = jnp.concatenate([turned[0:64], turned[64:128]], axis=1)
    shifts = lax.broadcasted_iota(jnp.int32, (WORDS, 32, QL), 1)
    bits = lax.shift_right_logical(
        jnp.broadcast_to(panel[:, None, :], (WORDS, 32, QL)), shifts) & 1
    bits = bits.reshape(NBITS, QL).astype(F32)
    scaled_count = alpha_weight * jnp.sum(bits, axis=0, keepdims=True)
    QQ[:, 0:QL] = bits.astype(F8)

    def step(i, carry):
        s = lax.rem(i, NBUF)
        lcp(i).wait()
        S[...] = jnp.dot(LB[s].astype(F8), QQ[...], preferred_element_type=F32)
        denominator = jnp.maximum(scaled_count + beta_weight * S[:, QL:2 * QL], 1.0)
        similarity = S[:, 0:QL] / denominator
        cutoffs = CB[pl.ds(pl.multiple_of(i * ROWS, ROWS), ROWS), :]
        hits = jax.nn.sigmoid(steepness * (similarity - cutoffs)).astype(BF)
        HT[...] = hits.T
        tcp(i).wait()
        for b in range(ROWS // BLOCK):
            block_hits = HT[:, b * BLOCK:(b + 1) * BLOCK]
            for k in range(0, KMAX, 2):
                slot = (i * (ROWS // BLOCK) + b) * KMAX + k
                pair = jnp.concatenate([TB[s, b, k], TB[s, b, k + 1]], axis=1)
                terms = jnp.dot(block_hits, pair, preferred_element_type=F32)
                C[slot] = terms[:, 0:TBLK] + C[tab[slot]]
                C[slot + 1] = terms[:, TBLK:2 * TBLK] + C[tab[slot + 1]]

        @pl.when(i + NBUF < STEPS)
        def _():
            lcp(i + NBUF).start()
            tcp(i + NBUF).start()

        return carry

    lax.fori_loop(0, STEPS, step, 0)

    def total(g, a, core_of, h):
        zz = lax.rem(z + ORDER[g] + 8, 8)
        yy = lax.rem(yl + a, 2)
        return C[tab[SLOTS + zz * 8 + yy * 4 + core_of * 2 + h]]

    mate = (qi, z * 4 + yl * 2 + (1 - core))
    beside = (qi, z * 4 + (1 - yl) * 2 + core)
    right, left = along(1), along(-1)

    swap = []
    for g in range(8):
        for a in range(2):
            for h in range(2):
                CS[g, a * 2 + h] = total(g, a, 1 - core, h)
        swap.append(start(remote(CS.at[g], CR.at[g], cs.at[g], cr.at[g], mate)))

    across = []
    ring0 = {}
    ring1 = {}

    def send0(d, a):
        n = RING0.index((d, a))
        ring0[d, a] = start(remote(
            M0.at[PLACE[d], a], R0.at[n], r0s.at[n], r0r.at[n], right))

    def send0l(d, a):
        n = RING0.index((d, 1 - a))
        ring0[-d, a] = start(remote(
            M0.at[PLACE[-d if d < 4 else 4], a], L0.at[n], l0s.at[n], l0r.at[n], left))

    def take0(d, a):
        n = RING0.index((d + 1, a))
        ring0[d + 1, a].wait_recv()
        g = PLACE[d]
        M0[g, a] = M0[g, a] + R0[n]

    def take0l(d, a):
        n = RING0.index((d + 1, 1 - a))
        ring0[-(d + 1), a].wait_recv()
        g = PLACE[-d]
        M0[g, a] = M0[g, a] + L0[n]

    def merge(g):
        swap[g].wait_recv()
        YS[g] = total(g, 1, core, 1) + CR[g, 3]
        across.append(start(remote(YS.at[g], YR.at[g], ys.at[g], yr.at[g], beside)))
        M0[g, 0] = total(g, 0, core, 0) + CR[g, 0]
        M0[g, 1] = total(g, 1, core, 0) + CR[g, 2]
        M1[g] = total(g, 0, core, 1) + CR[g, 1]

    def join(g):
        across[g].wait_recv()
        M1[g] = M1[g] + YR[g]

    def far1():
        g = PLACE[4]
        join(g)
        ring1[4] = start(remote(M1.at[g, pl.ds(0, 64)], R1H, r1s.at[3], r1r.at[3], right))
        ring1[-4] = start(remote(M1.at[g, pl.ds(64, 64)], L1H, l1s.at[3], l1r.at[3], left))

    def take1(d):
        g = PLACE[d]
        ring1[d + 1].wait_recv()
        if d == 3:
            M1[g, 0:64] = M1[g, 0:64] + R1H[...]
        else:
            M1[g] = M1[g] + R1[d]

    def take1l(d):
        g = PLACE[-d]
        ring1[-(d + 1)].wait_recv()
        if d == 3:
            M1[g, 64:128] = M1[g, 64:128] + L1H[...]
        else:
            M1[g] = M1[g] + L1[d]

    def send1(d):
        ring1[d] = start(remote(
            M1.at[PLACE[d]], R1.at[d - 1], r1s.at[d - 1], r1r.at[d - 1], right))

    def send1l(d):
        ring1[-d] = start(remote(
            M1.at[PLACE[-d]], L1.at[d - 1], l1s.at[d - 1], l1r.at[d - 1], left))

    merge(0)
    send0(4, 0)
    send0l(4, 1)
    merge(1)
    send0(3, 1)
    merge(2)
    send0l(3, 0)
    take0(3, 0)
    send0(3, 0)
    take0l(3, 1)
    send0l(3, 1)
    merge(3)
    merge(4)
    far1()
    merge(5)
    merge(6)
    merge(7)
    take0(2, 1)
    send0(2, 1)
    take0l(2, 0)
    send0l(2, 0)
    take0(2, 0)
    send0(2, 0)
    take0l(2, 1)
    send0l(2, 1)
    for d in (3,):
        join(PLACE[d])
        take1(d)
        send1(d)
        join(PLACE[-d])
        take1l(d)
        send1l(d)
    take0(1, 1)
    send0(1, 1)
    take0l(1, 0)
    send0l(1, 0)
    take0(1, 0)
    send0(1, 0)
    take0l(1, 1)
    send0l(1, 1)
    for d in (2,):
        join(PLACE[d])
        take1(d)
        send1(d)
        join(PLACE[-d])
        take1l(d)
        send1l(d)
    own = PLACE[0]
    take0(0, 1)
    take0l(0, 1)
    F0[...] = M0[own, 1]
    final = start(remote(F0, FY, fs, fr, beside))
    for d in (1,):
        join(PLACE[d])
        take1(d)
        send1(d)
        join(PLACE[-d])
        take1l(d)
        send1l(d)
    take0(0, 0)
    take0l(0, 0)
    join(own)
    final.wait_recv()
    M0[own, 0] = M0[own, 0] + FY[...]
    MS[0] = jnp.sum(M0[own, 0].reshape(16, 8, 128), axis=0)
    take1(0)
    take1l(0)
    MS[1] = jnp.sum(M1[own].reshape(16, 8, 128), axis=0)

    means = [start(remote(MS, MR.at[k], ms.at[k], mr.at[k], other(k + 1)))
             for k in range(7)]
    for copy in means:
        copy.wait_recv()
    sums = MS[...]
    for k in range(7):
        sums = sums + MR[k]
    mean = jnp.sum(sums, axis=1, keepdims=True) * (1.0 / 1024.0)
    for h in range(2):
        block = M0[own, 0] if h == 0 else M1[own]
        block = (block - mean[h]) * (1.0 / BLOCK)
        TMP[pl.ds(0, 64, stride=2), :] = block[0:64]
        TMP[pl.ds(1, 64, stride=2), :] = block[64:128]
        out[h * TBLK:(h + 1) * TBLK, :] = TMP[...].T
    for copy in sent:
        copy.wait_send()


def local(query_words, lib_bits, cutoff, counts, targets, activity_tiles):
    position = lax.rem(lax.axis_index("lib"), 4)
    packed = jnp.tile(query_words.reshape(2, 128), (4, 1))
    rows = lax.broadcasted_iota(jnp.int32, (8, 128), 0)
    words = jnp.where(rows // 2 == position, packed, 0)

    target = targets.reshape(SLOTS)
    live = (jnp.arange(KMAX, dtype=jnp.int32)[None, :] < counts[:, None]).reshape(SLOTS)
    key = jnp.where(live, target, -1)
    slot = jnp.arange(SLOTS, dtype=jnp.int32)
    wanted = jnp.concatenate([target, jnp.arange(64, dtype=jnp.int32)])
    bound = jnp.concatenate([slot, jnp.full((64,), SLOTS, jnp.int32)])
    named = (wanted[:, None] == key[None, :]) & (slot[None, :] < bound[:, None])
    tab = jnp.max(jnp.where(named, slot[None, :], -1), axis=1)
    tab = jnp.where(tab < 0, SLOTS, tab)

    V = pltpu.VMEM
    dma = pltpu.SemaphoreType.DMA
    block = (QL, TBLK)
    return pl.pallas_call(
        kernel,
        out_shape=jax.ShapeDtypeStruct((2 * TBLK, QL), F32),
        in_specs=[
            pl.BlockSpec(memory_space=pltpu.SMEM),
            pl.BlockSpec(memory_space=V),
            pl.BlockSpec(memory_space=V),
            pl.BlockSpec(memory_space=pl.ANY),
            pl.BlockSpec(memory_space=pl.ANY),
        ],
        out_specs=pl.BlockSpec(memory_space=V),
        scratch_shapes=[
            V((NBITS, 2 * QL), F8),
            V((NBUF, ROWS, NBITS), BF),
            V((NBUF, ROWS // BLOCK, KMAX, BLOCK, TBLK), BF),
            V((ROWS, 2 * QL), F32),
            V((QL, ROWS), BF),
            V((SLOTS + 1,) + block, F32),
            V((LIB, 128), F32),
            V((8, 128), jnp.int32),
            V((3, 8, 128), jnp.int32),
            V((8, 8, 128), jnp.int32),
            V((8, 4) + block, F32),
            V((8, 4) + block, F32),
            V((8, 2) + block, F32),
            V((8,) + block, F32),
            V((8,) + block, F32),
            V((8,) + block, F32),
            V(block, F32),
            V(block, F32),
            V((7,) + block, F32),
            V((7,) + block, F32),
            V((64, TBLK), F32),
            V((64, TBLK), F32),
            V((3,) + block, F32),
            V((3,) + block, F32),
            V((2, 8, 128), F32),
            V((7, 2, 8, 128), F32),
            V(block, F32),
            dma((NBUF,)), dma((NBUF,)),
            dma((3,)), dma((3,)), dma((7,)), dma((7,)),
            dma((8,)), dma((8,)), dma((8,)), dma((8,)),
            dma, dma,
            dma((7,)), dma((7,)), dma((7,)), dma((7,)),
            dma((4,)), dma((4,)), dma((4,)), dma((4,)),
            dma((7,)), dma((7,)),
        ],
        compiler_params=pltpu.CompilerParams(
            collective_id=0, has_side_effects=True, vmem_limit_bytes=60 * 2**20),
        cost_estimate=pl.CostEstimate(
            flops=2 * LIB * NBITS * 2 * QL, bytes_accessed=48 * 2**20,
            transcendentals=LIB * QL),
        name="screen",
    )(tab, words, cutoff.reshape(LIB // 128, 128), lib_bits, activity_tiles)


def solution(mesh):
    in_specs = (
        P(("query", "lib"), None),
        P("lib", None),
        P("lib"),
        P("lib"),
        P("lib", None),
        P("lib", None, None, None),
    )
    out_specs = P("lib", "query")
    return jax.shard_map(local, mesh=mesh, in_specs=in_specs, out_specs=out_specs, check_vma=False)
```

time: 270 us -> 67.2 us (0.25); the launches traced: 264 us -> 67 us
  waiting for transfers between devices: 117 us -> 0 us
  Pallas kernels: 0 us -> 60.8 us
  blocking collectives: 59.1 us -> 0 us
  matrix products: 45.2 us -> 0 us
  between operations: 13.5 us -> 0.05 us
  local copies, waits for them, and re-layouts: 15.4 us -> 3.28 us
  other arithmetic: 14.6 us -> 2.88 us
    reduce_scatter x1 -> x0, waiting for transfers between devices: 117 us -> none  [local(): lax.psum_scatter(partial_scores, 'lib', scatter_dimension=0, tiled=True)]
    pallas_call x0 -> x1, Pallas kernels: none -> 60.8 us  [local(): pl.pallas_call(kernel, out_shape=jax.ShapeDtypeStruct((2 * TBLK, QL), F32...]
    dot_general x3 -> x0, matrix products: 45.2 us -> none  [the longest x1 17.2 us: screen(): lax.dot_general(lib_bits, query_bits, (((1,), (1,)), ((), ())), preferred...]
    all_gather x1 -> x0, blocking collectives: 38.9 us -> none  [local(): panel_words = lax.all_gather(query_words, 'lib', axis=0, tiled=True)]
    psum x1 -> x0, blocking collectives: 20.2 us -> none  [local(): target_total = lax.psum(colsum, 'query')]
    reduce_sum x3 -> x0, other arithmetic: 12.5 us -> none  [the longest x1 11.2 us: local(): library_count = jnp.sum(lib_bits, axis=1, dtype=jnp.float32)]
    dot_general x1 -> x0, local copies, waits for them, and re-layouts: 9.3 us -> none  [local(): jnp.einsum('bkiu,biq->bkuq', activity_tiles, block_hits, preferred_elemen...]
    reshape x1, local copies, waits for them, and re-layouts: 4.87 us -> 0.09 us  [local(): target = targets.reshape(SLOTS)]
  transfers between devices with their start and end apart: 1 -> 0, of which waited for: 1 -> 0; matrix products, arithmetic and copies ran while one was open for 0% -> 0% of each run, Pallas kernels for 0% -> 0%
where the time goes in v1:
time: 67.2 us; the launch traced here: 67 us
  Pallas kernels  60.8 us (90%)
  local copies, waits for them, and re-layouts  3.28 us (5%)
  other arithmetic  2.88 us (4%)
    pallas_call x1, Pallas kernels, local(): pl.pallas_call(kernel, out_shape=jax.ShapeDtypeStruct((2 * TBLK, QL), F32...  60.8 us
    unnamed x2, local copies, waits for them, and re-layouts  2.33 us

profile of v1, /device:TPU:1, one launch (start us, length us, event | category | flops | bytes accessed | tf_op | source)
XLA Modules:
  0.0 67.0 jit_solution(8726887082767430858)
XLA Ops:
  0.0 0.8 %tile.10 = s32[2,128]{1,0:T(2,128)S(1)} reshape(s32[4,64]{1,0:T(4,128)} %param.6) | data formatting | bytes 2048 | tf_op jit(solution)/shard_map/tile | solution.py:321
  0.8 0.7 %iota_compare_fusion.1 = pred[16,8]{1,0:T(8,128)(4,1)S(1)} fusion(s32[16]{0:T(128)} %param.9), kind=kLoop, calls=%fused_computation.3 | loop fusion | flops 128 | bytes 192 | tf_op jit(solution)/shard_map/lt | solution.py:326
  1.5 0.1 lt.45
  1.6 0.7 %fusion.1.words = s32[8,128]{1,0:T(8,128)} fusion(s32[8,128]{1,0:T(8,128)S(1)} %bitcast.3, s32[]{:T(128)S(6)} %rem.26, s32[8]{0:T(128)S(1)} %get-tuple-element.5, s32[8]{0:T(128)S(1)} %get-tuple-element.6, pred[8]{0:T(512)(128)(4,1)S(1)} %compare_and_fusion), kind=kLoop, calls=%fused_computation.5 | loop fusion | flops 3072 | bytes 8268 | tf_op jit(solution)/shard_map/jit(_where)/select_n | solution.py:323
  2.3 0.8 %copy.9 = s32[16,8]{1,0:T(8,128)S(1)} copy(s32[16,8]{0,1:T(8,128)} %param.10) | data formatting | bytes 1024 | tf_op args[4]
  3.1 0.1 reshape.31
  3.2 0.9 %select_reduce_fusion = s32[192]{0:T(256)S(1)} fusion(s32[192]{0:T(256)} %constant.29.clone.1, s32[128]{0:T(128)S(1)} %broadcast_select_fusion, s32[192]{0:T(256)S(1)} %pad_add_fusion), kind=kLoop, calls=%fused_computation | loop fusion | flops 122688 | bytes 2816 | tf_op jit(solution)/shard_map/reduce_max | solution.py:332
  4.1 0.6 compare_select_fusion.tab
  4.6 60.8 %screen.1 = f32[256,128]{1,0:T(8,128)} custom-call(s32[192]{0:T(256)} %compare_select_fusion.tab, s32[8,128]{1,0:T(8,128)} %fusion.1.words, f32[64,128]{1,0:T(8,128)} %bitcast.2, bf16[8192,2048]{1,0:T(8,128)(2,1)} %lib.1, bf16[16,8,512,128]{3,2,1,0:T(8,128)(2,1)} %tiles.1), custom_call_target="tpu_custom_call" | custom-call | flops 8589934592 | bytes 50331648 | tf_op jit(solution)/shard_map/screen/pallas_call | solution.py:338
  65.4 1.6 %copy.11 = f32[256,128]{1,0:T(8,128)} copy(f32[256,128]{1,0:T(8,128)} %screen.1) | data formatting | bytes 262144
  (6 shorter events, 0.0 us)

commit v2 on v1

--- a/solution.py
+++ b/solution.py
@@ -31,10 +31,10 @@
 RING0 = ((4, 0), (3, 1), (3, 0), (2, 1), (2, 0), (1, 1), (1, 0))
 
 
-def kernel(tab, words, cut, lib, tiles, out,
-           QQ, LB, TB, S, HT, C, CB, W1, WR, G, CS, CR, M0, M1, YS, YR, F0, FY,
+def kernel(query_words, cutoff, counts, targets, lib, tiles, out,
+           QQ, LB, TB, S, HT, C, W0, CUT, CN, TG, TABV, tab, W, W1, WR, G, CS, CR, M0, M1, YS, YR, F0, FY,
            R0, L0, R1H, L1H, R1, L1, MS, MR, TMP,
-           lsem, tsem, g1s, g1r, g2s, g2r, cs, cr, ys, yr, fs, fr,
+           lsem, tsem, isem, tabsem, g1s, g1r, g2s, g2r, cs, cr, ys, yr, fs, fr,
            r0s, r0r, l0s, l0r, r1s, r1r, l1s, l1r, ms, mr):
     qi = lax.axis_index("query")
     li = lax.axis_index("lib")
@@ -53,9 +53,15 @@
         return pltpu.make_async_copy(
             tiles.at[pl.ds(i * (ROWS // BLOCK), ROWS // BLOCK)], TB.at[s], tsem.at[s])
 
-    for i in range(NBUF):
+    small = [pltpu.make_async_copy(src, dst, isem.at[n]) for n, (src, dst) in enumerate((
+        (query_words, W0), (counts, CN), (targets, TG), (cutoff, CUT)))]
+    for copy in small:
+        copy.start()
+    lcp(0).start()
+    for i in range(1, NBUF):
         lcp(i).start()
-        tcp(i).start()
+        tcp(i - 1).start()
+    tcp(NBUF - 1).start()
 
     def square(k):
         return (qi, z * 4 + lax.rem(p4 + k, 4))
@@ -86,25 +92,52 @@
         sent.append(copy)
         return copy
 
-    one = [start(remote(words, WR.at[k], g1s.at[k], g1r.at[k], square(k + 1)))
+    small[0].wait()
+    rows = lax.broadcasted_iota(jnp.int32, (8, 128), 0)
+    W[...] = jnp.zeros((8, 128), jnp.int32)
+    for j in range(2):
+        row = jnp.concatenate([W0[2 * j:2 * j + 1], W0[2 * j + 1:2 * j + 2]], axis=1)
+        W[...] = jnp.where(rows == 2 * p4 + j, jnp.broadcast_to(row, (8, 128)), W[...])
+    one = [start(remote(W, WR.at[k], g1s.at[k], g1r.at[k], square(k + 1)))
            for k in range(3)]
 
-    def cutstep(r, carry):
-        for k in range(4):
-            row = r * 4 + k
-            CB[pl.ds(pl.multiple_of(row * 128, 128), 128), :] = jnp.broadcast_to(
-                cut[pl.ds(row, 1), :], (128, 128)).T
-        return carry
+    small[1].wait()
+    small[2].wait()
+    small[3].wait()
+    blocks = SLOTS // KMAX
+    of_block = (lax.broadcasted_iota(jnp.int32, (SLOTS, blocks), 0) // KMAX
+                == lax.broadcasted_iota(jnp.int32, (SLOTS, blocks), 1)).astype(F32)
+    spread = lax.dot_general(of_block, TG[...].astype(F32), (((1,), (1,)), ((), ())),
+                             preferred_element_type=F32)
+    place = lax.broadcasted_iota(jnp.int32, (SLOTS, KMAX), 0) % KMAX
+    number = lax.broadcasted_iota(jnp.int32, (SLOTS, KMAX), 1)
+    target = jnp.sum(jnp.where(place == number, spread, 0.0), axis=1, keepdims=True)
+    live = jnp.sum(of_block * CN[...].astype(F32), axis=1, keepdims=True)
+    slot_place = (lax.broadcasted_iota(jnp.int32, (SLOTS, 1), 0) % KMAX).astype(F32)
+    key = jnp.where(slot_place < live, target, -1.0)
+    keys = jnp.broadcast_to(key, (SLOTS, SLOTS))
+    wanted = jnp.broadcast_to(target, (SLOTS, SLOTS)).T
+    down = lax.broadcasted_iota(jnp.int32, (SLOTS, SLOTS), 0)
+    over = lax.broadcasted_iota(jnp.int32, (SLOTS, SLOTS), 1)
+    before = jnp.max(jnp.where((keys == wanted) & (down < over), down, -1),
+                     axis=0, keepdims=True)
+    final_slot = jnp.max(jnp.where(keys == over.astype(F32), down, -1),
+                         axis=0, keepdims=True)
+    both = jnp.where(rows == 0, jnp.broadcast_to(before, (8, 128)),
+                     jnp.broadcast_to(final_slot, (8, 128)))
+    TABV[...] = jnp.where(both < 0, SLOTS, both)
+    tabcopy = pltpu.make_async_copy(TABV, tab, tabsem)
+    tabcopy.start()
 
     for copy in one:
         copy.wait_recv()
-    W1[...] = words[...] + WR[0] + WR[1] + WR[2]
+    W1[...] = W[...] + WR[0] + WR[1] + WR[2]
     two = [start(remote(W1, G.at[z], g2s.at[k], g2r.at[k], along(k + 1)))
            for k in range(7)]
     G[z] = W1[...]
     C[SLOTS] = jnp.zeros((QL, TBLK), F32)
     QQ[:, QL:2 * QL] = jnp.ones((NBITS, QL), F32).astype(F8)
-    lax.fori_loop(0, 16, cutstep, 0)
+    tabcopy.wait()
     for copy in two:
         copy.wait_recv()
 
@@ -117,38 +150,66 @@
     scaled_count = alpha_weight * jnp.sum(bits, axis=0, keepdims=True)
     QQ[:, 0:QL] = bits.astype(F8)
 
-    def step(i, carry):
-        s = lax.rem(i, NBUF)
-        lcp(i).wait()
-        S[...] = jnp.dot(LB[s].astype(F8), QQ[...], preferred_element_type=F32)
+    def screen(i, S):
+        S[...] = jnp.dot(LB[lax.rem(i, NBUF)].astype(F8), QQ[...],
+                         preferred_element_type=F32)
+
+    def hit(i, S, HT):
         denominator = jnp.maximum(scaled_count + beta_weight * S[:, QL:2 * QL], 1.0)
         similarity = S[:, 0:QL] / denominator
-        cutoffs = CB[pl.ds(pl.multiple_of(i * ROWS, ROWS), ROWS), :]
+        cutoffs = jnp.concatenate(
+            [jnp.broadcast_to(CUT[pl.ds(i * (ROWS // 128) + k, 1), :], (128, 128)).T
+             for k in range(ROWS // 128)], axis=0)
         hits = jax.nn.sigmoid(steepness * (similarity - cutoffs)).astype(BF)
         HT[...] = hits.T
-        tcp(i).wait()
+
+    def gather_terms(i, HT):
+        s = lax.rem(i, NBUF)
         for b in range(ROWS // BLOCK):
             block_hits = HT[:, b * BLOCK:(b + 1) * BLOCK]
             for k in range(0, KMAX, 2):
                 slot = (i * (ROWS // BLOCK) + b) * KMAX + k
                 pair = jnp.concatenate([TB[s, b, k], TB[s, b, k + 1]], axis=1)
                 terms = jnp.dot(block_hits, pair, preferred_element_type=F32)
-                C[slot] = terms[:, 0:TBLK] + C[tab[slot]]
-                C[slot + 1] = terms[:, TBLK:2 * TBLK] + C[tab[slot + 1]]
+                C[slot] = terms[:, 0:TBLK] + C[tab[0, slot]]
+                C[slot + 1] = terms[:, TBLK:2 * TBLK] + C[tab[0, slot + 1]]
+
+    Ss = (S.at[0], S.at[1])
+    HTs = (HT.at[0], HT.at[1])
+    lcp(0).wait()
+    screen(0, Ss[0])
+    lcp(NBUF).start()
+    hit(0, Ss[0], HTs[0])
+
+    def advance(i, u):
+        lcp(i + 1).wait()
+        tcp(i).wait()
+        screen(i + 1, Ss[1 - u])
+        gather_terms(i, HTs[u])
+        hit(i + 1, Ss[1 - u], HTs[1 - u])
+
+        @pl.when(i + 1 + NBUF < STEPS)
+        def _():
+            lcp(i + 1 + NBUF).start()
 
         @pl.when(i + NBUF < STEPS)
         def _():
-            lcp(i + NBUF).start()
             tcp(i + NBUF).start()
 
+    def twice(j, carry):
+        advance(2 * j, 0)
+        advance(2 * j + 1, 1)
         return carry
 
-    lax.fori_loop(0, STEPS, step, 0)
+    lax.fori_loop(0, STEPS // 2 - 1, twice, 0)
+    advance(STEPS - 2, 0)
+    tcp(STEPS - 1).wait()
+    gather_terms(STEPS - 1, HTs[1])
 
     def total(g, a, core_of, h):
         zz = lax.rem(z + ORDER[g] + 8, 8)
         yy = lax.rem(yl + a, 2)
-        return C[tab[SLOTS + zz * 8 + yy * 4 + core_of * 2 + h]]
+        return C[tab[1, zz * 8 + yy * 4 + core_of * 2 + h]]
 
     mate = (qi, z * 4 + yl * 2 + (1 - core))
     beside = (qi, z * 4 + (1 - yl) * 2 + core)
@@ -317,43 +378,28 @@
 
 
 def local(query_words, lib_bits, cutoff, counts, targets, activity_tiles):
-    position = lax.rem(lax.axis_index("lib"), 4)
-    packed = jnp.tile(query_words.reshape(2, 128), (4, 1))
-    rows = lax.broadcasted_iota(jnp.int32, (8, 128), 0)
-    words = jnp.where(rows // 2 == position, packed, 0)
-
-    target = targets.reshape(SLOTS)
-    live = (jnp.arange(KMAX, dtype=jnp.int32)[None, :] < counts[:, None]).reshape(SLOTS)
-    key = jnp.where(live, target, -1)
-    slot = jnp.arange(SLOTS, dtype=jnp.int32)
-    wanted = jnp.concatenate([target, jnp.arange(64, dtype=jnp.int32)])
-    bound = jnp.concatenate([slot, jnp.full((64,), SLOTS, jnp.int32)])
-    named = (wanted[:, None] == key[None, :]) & (slot[None, :] < bound[:, None])
-    tab = jnp.max(jnp.where(named, slot[None, :], -1), axis=1)
-    tab = jnp.where(tab < 0, SLOTS, tab)
-
     V = pltpu.VMEM
     dma = pltpu.SemaphoreType.DMA
     block = (QL, TBLK)
     return pl.pallas_call(
         kernel,
         out_shape=jax.ShapeDtypeStruct((2 * TBLK, QL), F32),
-        in_specs=[
-            pl.BlockSpec(memory_space=pltpu.SMEM),
-            pl.BlockSpec(memory_space=V),
-            pl.BlockSpec(memory_space=V),
-            pl.BlockSpec(memory_space=pl.ANY),
-            pl.BlockSpec(memory_space=pl.ANY),
-        ],
+        in_specs=[pl.BlockSpec(memory_space=pl.ANY)] * 6,
         out_specs=pl.BlockSpec(memory_space=V),
         scratch_shapes=[
             V((NBITS, 2 * QL), F8),
             V((NBUF, ROWS, NBITS), BF),
             V((NBUF, ROWS // BLOCK, KMAX, BLOCK, TBLK), BF),
-            V((ROWS, 2 * QL), F32),
-            V((QL, ROWS), BF),
+            V((2, ROWS, 2 * QL), F32),
+            V((2, QL, ROWS), BF),
             V((SLOTS + 1,) + block, F32),
-            V((LIB, 128), F32),
+            V((4, WORDS), jnp.int32),
+            V((LIB // 128, 128), F32),
+            V((1, SLOTS // KMAX), jnp.int32),
+            V((KMAX, SLOTS // KMAX), jnp.int32),
+            V((8, 128), jnp.int32),
+            pltpu.SMEM((8, 128), jnp.int32),
+            V((8, 128), jnp.int32),
             V((8, 128), jnp.int32),
             V((3, 8, 128), jnp.int32),
             V((8, 8, 128), jnp.int32),
@@ -374,7 +420,7 @@
             V((2, 8, 128), F32),
             V((7, 2, 8, 128), F32),
             V(block, F32),
-            dma((NBUF,)), dma((NBUF,)),
+            dma((NBUF,)), dma((NBUF,)), dma((4,)), dma,
             dma((3,)), dma((3,)), dma((7,)), dma((7,)),
             dma((8,)), dma((8,)), dma((8,)), dma((8,)),
             dma, dma,
@@ -388,7 +434,8 @@
             flops=2 * LIB * NBITS * 2 * QL, bytes_accessed=48 * 2**20,
             transcendentals=LIB * QL),
         name="screen",
-    )(tab, words, cutoff.reshape(LIB // 128, 128), lib_bits, activity_tiles)
+    )(query_words, cutoff.reshape(LIB // 128, 128), counts.reshape(1, SLOTS // KMAX),
+      targets.T, lib_bits, activity_tiles)
 
 
 def solution(mesh):

time: 67.2 us -> 58.7 us (0.87)
  Pallas kernels: 60.8 us -> 57 us
  other arithmetic: 2.88 us -> 0 us
  local copies, waits for them, and re-layouts: 3.28 us -> 1.57 us
    pallas_call x1, Pallas kernels: 60.8 us -> 57 us  [local(): pl.pallas_call(kernel, out_shape=jax.ShapeDtypeStruct((2 * TBLK, QL), F32...]
    select_n x3 -> x0, other arithmetic: 1.25 us -> none  [the longest x1 0.67 us: local(): words = jnp.where(rows // 2 == position, packed, 0)]
    reduce_max x1 -> x0, other arithmetic: 0.88 us -> none  [local(): tab = jnp.max(jnp.where(named, slot[None, :], -1), axis=1)]
    another operation x2 -> x0, local copies, waits for them, and re-layouts: 0.77 us -> none  [local(): packed = jnp.tile(query_words.reshape(2, 128), (4, 1))]
    unnamed x2 -> x1, local copies, waits for them, and re-layouts: 2.33 us -> 1.57 us
    lt x1 -> x0, other arithmetic: 0.73 us -> none  [local(): jnp.arange(KMAX, dtype=jnp.int32)[None, :] < counts[:, None]]
where the time goes in v2:
time: 58.7 us; the launch traced here: 58.6 us
  Pallas kernels  57 us (97%)
  local copies, waits for them, and re-layouts  1.57 us (3%)
    pallas_call x1, Pallas kernels, local(): pl.pallas_call(kernel, out_shape=jax.ShapeDtypeStruct((2 * TBLK, QL), F32...  57 us
    unnamed x1, local copies, waits for them, and re-layouts  1.57 us

profile of v2, /device:TPU:1, one launch (start us, length us, event | category | flops | bytes accessed | tf_op | source)
XLA Modules:
  0.0 58.6 jit_solution(16246520911664531818)
XLA Ops:
  0.0 57.0 %screen.1 = f32[256,128]{1,0:T(8,128)} custom-call(s32[4,64]{1,0:T(4,128)} %query_words.1, f32[64,128]{1,0:T(8,128)} %bitcast.3, s32[1,16]{1,0:T(1,128)} %bitcast.5, s32[8,16]{1,0:T(8,128)} %bitcast.4, bf16[8192,2048]{1,0:T(8,128)(2,1)} %lib.1, bf16[16,8,512,128]{3,2,1,0:T(8,128)(2,1)} %tiles.1), custom_call_target="tpu_custom_call" | custom-call | flops 8589934592 | bytes 50331648 | tf_op jit(solution)/shard_map/screen/pallas_call | solution.py:384
  57.0 1.6 %copy.8 = f32[256,128]{1,0:T(8,128)} copy(f32[256,128]{1,0:T(8,128)} %screen.1) | data formatting | bytes 262144

commit v3 on v2

--- a/solution.py
+++ b/solution.py
@@ -11,7 +11,7 @@
 NBITS = 2048
 WORDS = 64
 ROWS = 1024
-NBUF = 4
+NBUF = 5
 LIB = 8192
 STEPS = LIB // ROWS
 SLOTS = LIB // BLOCK * KMAX
@@ -28,14 +28,24 @@
 
 ORDER = (4, 3, -3, 2, -2, 1, -1, 0)
 PLACE = {d: g for g, d in enumerate(ORDER)}
-RING0 = ((4, 0), (3, 1), (3, 0), (2, 1), (2, 0), (1, 1), (1, 0))
+HALF = 64
+
+STEPS_OF_SUM = (
+    "S0", "S1", "S2", "S3", "S4", "S5", "S6", "S7", "M0", "L42", "R41", "R40", "L43", "M1",
+    "R33", "R32", "M2", "L30", "L31", "M3", "M4", "M5", "M6", "M7", "C1", "J00", "L32", "R31",
+    "Rh40", "J01", "Lh41", "L33", "R30", "J10", "L20", "R23", "J11", "Rh31", "L21", "R22",
+    "J20", "Lh30", "L22", "R21", "J21", "Lh31", "J30", "Rh30", "L23", "R20", "J31", "C2",
+    "L10", "J40", "R13", "L11", "J41", "Rh21", "Lh20", "J50", "R12", "L12", "J51", "R11",
+    "Lh21", "Rh20", "J60", "C3", "L13", "J61", "R10", "J70", "J71", "Rh11", "Lh10", "F2",
+    "Lh11", "Rh10", "F3", "E00", "E01", "E10", "E11",
+)
 
 
 def kernel(query_words, cutoff, counts, targets, lib, tiles, out,
-           QQ, LB, TB, S, HT, C, W0, CUT, CN, TG, TABV, tab, W, W1, WR, G, CS, CR, M0, M1, YS, YR, F0, FY,
-           R0, L0, R1H, L1H, R1, L1, MS, MR, TMP,
+           QQ, LB, TB, S, HT, C, W0, CUT, CN, TG, TABV, tab, W, W1, WR, G, CS, CR, M0, M1, YS, YR, FY,
+           R0, L0, R1, L1, MC, MZ, MX, MY, TMP,
            lsem, tsem, isem, tabsem, g1s, g1r, g2s, g2r, cs, cr, ys, yr, fs, fr,
-           r0s, r0r, l0s, l0r, r1s, r1r, l1s, l1r, ms, mr):
+           r0s, r0r, l0s, l0r, r1s, r1r, l1s, l1r, zs, zr, xs, xr, us, ur):
     qi = lax.axis_index("query")
     li = lax.axis_index("lib")
     z = li // 4
@@ -58,10 +68,7 @@
     for copy in small:
         copy.start()
     lcp(0).start()
-    for i in range(1, NBUF):
-        lcp(i).start()
-        tcp(i - 1).start()
-    tcp(NBUF - 1).start()
+    lcp(1).start()
 
     def square(k):
         return (qi, z * 4 + lax.rem(p4 + k, 4))
@@ -69,16 +76,22 @@
     def along(k):
         return (qi, lax.rem(z + k + 8, 8) * 4 + p4)
 
-    def other(k):
-        return (lax.rem(qi + k, 8), li)
+    def aside(k):
+        return (lax.rem(qi + 2 * k, 8), li)
+
+    high = lax.rem(qi, 2)
+    beside = (qi, z * 4 + (1 - yl) * 2 + core)
+    over_y = (beside,
+              (qi + 1 - 2 * high, li),
+              (qi + 1 - 2 * high, z * 4 + (1 - yl) * 2 + core))
 
     partners = [square(k) for k in (1, 2, 3)]
     partners += [along(k) for k in range(1, 8)]
-    partners += [other(k) for k in range(1, 8)]
+    partners += [aside(k) for k in range(1, 4)]
+    partners += over_y[1:]
     barrier = pltpu.get_barrier_semaphore()
     for dev in partners:
         pl.semaphore_signal(barrier, inc=1, device_id=dev, device_id_type=MESH)
-    pl.semaphore_wait(barrier, len(partners))
 
     def remote(src, dst, ssem, rsem, dev):
         return pltpu.make_async_remote_copy(
@@ -92,18 +105,10 @@
         sent.append(copy)
         return copy
 
-    small[0].wait()
-    rows = lax.broadcasted_iota(jnp.int32, (8, 128), 0)
-    W[...] = jnp.zeros((8, 128), jnp.int32)
-    for j in range(2):
-        row = jnp.concatenate([W0[2 * j:2 * j + 1], W0[2 * j + 1:2 * j + 2]], axis=1)
-        W[...] = jnp.where(rows == 2 * p4 + j, jnp.broadcast_to(row, (8, 128)), W[...])
-    one = [start(remote(W, WR.at[k], g1s.at[k], g1r.at[k], square(k + 1)))
-           for k in range(3)]
-
     small[1].wait()
     small[2].wait()
     small[3].wait()
+    rows = lax.broadcasted_iota(jnp.int32, (8, 128), 0)
     blocks = SLOTS // KMAX
     of_block = (lax.broadcasted_iota(jnp.int32, (SLOTS, blocks), 0) // KMAX
                 == lax.broadcasted_iota(jnp.int32, (SLOTS, blocks), 1)).astype(F32)
@@ -129,6 +134,20 @@
     tabcopy = pltpu.make_async_copy(TABV, tab, tabsem)
     tabcopy.start()
 
+    tcp(0).start()
+    for i in range(2, NBUF):
+        lcp(i).start()
+        tcp(i - 1).start()
+    tcp(NBUF - 1).start()
+
+    small[0].wait()
+    W[...] = jnp.zeros((8, 128), jnp.int32)
+    for j in range(2):
+        row = jnp.concatenate([W0[2 * j:2 * j + 1], W0[2 * j + 1:2 * j + 2]], axis=1)
+        W[...] = jnp.where(rows == 2 * p4 + j, jnp.broadcast_to(row, (8, 128)), W[...])
+    pl.semaphore_wait(barrier, len(partners))
+    one = [start(remote(W, WR.at[k], g1s.at[k], g1r.at[k], square(k + 1)))
+           for k in range(3)]
     for copy in one:
         copy.wait_recv()
     W1[...] = W[...] + WR[0] + WR[1] + WR[2]
@@ -179,14 +198,13 @@
     lcp(0).wait()
     screen(0, Ss[0])
     lcp(NBUF).start()
-    hit(0, Ss[0], HTs[0])
 
     def advance(i, u):
         lcp(i + 1).wait()
         tcp(i).wait()
+        hit(i, Ss[u], HTs[u])
         screen(i + 1, Ss[1 - u])
         gather_terms(i, HTs[u])
-        hit(i + 1, Ss[1 - u], HTs[1 - u])
 
         @pl.when(i + 1 + NBUF < STEPS)
         def _():
@@ -204,6 +222,7 @@
     lax.fori_loop(0, STEPS // 2 - 1, twice, 0)
     advance(STEPS - 2, 0)
     tcp(STEPS - 1).wait()
+    hit(STEPS - 1, Ss[1], HTs[1])
     gather_terms(STEPS - 1, HTs[1])
 
     def total(g, a, core_of, h):
@@ -212,164 +231,128 @@
         return C[tab[1, zz * 8 + yy * 4 + core_of * 2 + h]]
 
     mate = (qi, z * 4 + yl * 2 + (1 - core))
-    beside = (qi, z * 4 + (1 - yl) * 2 + core)
     right, left = along(1), along(-1)
 
-    swap = []
-    for g in range(8):
+    swap, across, ring, last, sums = {}, {}, {}, {}, {}
+    own = PLACE[0]
+    low = {0: pl.ds(0, HALF), 1: pl.ds(HALF, HALF)}
+
+    def step_S(g):
         for a in range(2):
             for h in range(2):
                 CS[g, a * 2 + h] = total(g, a, 1 - core, h)
-        swap.append(start(remote(CS.at[g], CR.at[g], cs.at[g], cr.at[g], mate)))
-
-    across = []
-    ring0 = {}
-    ring1 = {}
-
-    def send0(d, a):
-        n = RING0.index((d, a))
-        ring0[d, a] = start(remote(
-            M0.at[PLACE[d], a], R0.at[n], r0s.at[n], r0r.at[n], right))
-
-    def send0l(d, a):
-        n = RING0.index((d, 1 - a))
-        ring0[-d, a] = start(remote(
-            M0.at[PLACE[-d if d < 4 else 4], a], L0.at[n], l0s.at[n], l0r.at[n], left))
-
-    def take0(d, a):
-        n = RING0.index((d + 1, a))
-        ring0[d + 1, a].wait_recv()
-        g = PLACE[d]
-        M0[g, a] = M0[g, a] + R0[n]
-
-    def take0l(d, a):
-        n = RING0.index((d + 1, 1 - a))
-        ring0[-(d + 1), a].wait_recv()
-        g = PLACE[-d]
-        M0[g, a] = M0[g, a] + L0[n]
-
-    def merge(g):
+        swap[g] = start(remote(CS.at[g], CR.at[g], cs.at[g], cr.at[g], mate))
+
+    def by_query(block):
+        return jnp.sum(block.reshape(QL // 8, 8, TBLK), axis=0, keepdims=True)
+
+    def step_M(g):
         swap[g].wait_recv()
-        YS[g] = total(g, 1, core, 1) + CR[g, 3]
-        across.append(start(remote(YS.at[g], YR.at[g], ys.at[g], yr.at[g], beside)))
-        M0[g, 0] = total(g, 0, core, 0) + CR[g, 0]
-        M0[g, 1] = total(g, 1, core, 0) + CR[g, 2]
-        M1[g] = total(g, 0, core, 1) + CR[g, 1]
-
-    def join(g):
-        across[g].wait_recv()
-        M1[g] = M1[g] + YR[g]
-
-    def far1():
-        g = PLACE[4]
-        join(g)
-        ring1[4] = start(remote(M1.at[g, pl.ds(0, 64)], R1H, r1s.at[3], r1r.at[3], right))
-        ring1[-4] = start(remote(M1.at[g, pl.ds(64, 64)], L1H, l1s.at[3], l1r.at[3], left))
-
-    def take1(d):
-        g = PLACE[d]
-        ring1[d + 1].wait_recv()
-        if d == 3:
-            M1[g, 0:64] = M1[g, 0:64] + R1H[...]
+        far = total(g, 1, core, 1) + CR[g, 3]
+        YS[g] = far
+        for h in range(2):
+            across[g, h] = start(remote(
+                YS.at[g, low[h]], YR.at[g, low[h]], ys.at[g, h], yr.at[g, h], beside))
+        near0 = total(g, 0, core, 0) + CR[g, 0]
+        near1 = total(g, 1, core, 0) + CR[g, 2]
+        kept = total(g, 0, core, 1) + CR[g, 1]
+        M0[g, 0] = near0
+        M0[g, 1] = near1
+        M1[g] = kept
+        MC[g, 0:4] = jnp.sum(jnp.concatenate(
+            [by_query(near0), by_query(kept), by_query(near1), by_query(far)], axis=0), axis=1)
+
+    def step_J(g, h):
+        across[g, h].wait_recv()
+        M1[g, low[h]] = M1[g, low[h]] + YR[g, low[h]]
+
+    def along_z(way, d, p):
+        sign = 1 if way == "R" else -1
+        g = PLACE[sign * d if d < 4 else 4]
+        buf, ssem, rsem = (R0, r0s, r0r) if way == "R" else (L0, l0s, l0r)
+        here = M0.at[g, p // 2, low[p % 2]]
+        before = ring.get((way, d + 1, p))
+        if before is not None:
+            before.wait_recv()
+            here[...] = here[...] + buf[d, p]
+        if d > 0:
+            ring[way, d, p] = start(remote(
+                here, buf.at[d - 1, p], ssem.at[d - 1, p], rsem.at[d - 1, p],
+                right if way == "R" else left))
+
+    def along_zh(way, d, h):
+        sign = 1 if way == "R" else -1
+        g = PLACE[sign * d if d < 4 else 4]
+        buf, ssem, rsem = (R1, r1s, r1r) if way == "R" else (L1, l1s, l1r)
+        here = M1.at[g, low[h]]
+        before = ring.get((way + "h", d + 1, h))
+        if before is not None:
+            before.wait_recv()
+            here[...] = here[...] + buf[d, h]
+        if d > 0:
+            ring[way + "h", d, h] = start(remote(
+                here, buf.at[d - 1, h], ssem.at[d - 1, h], rsem.at[d - 1, h],
+                right if way == "R" else left))
+
+    def step_F(p):
+        along_z("R", 0, p)
+        along_z("L", 0, p)
+        if p >= 2:
+            last[p] = start(remote(
+                M0.at[own, 1, low[p - 2]], FY.at[low[p - 2]], fs.at[p - 2], fr.at[p - 2],
+                beside))
+
+    def step_E(h, part):
+        if h == 0:
+            step_F(part)
+            last[part + 2].wait_recv()
+            M0[own, 0, low[part]] = M0[own, 0, low[part]] + FY[low[part]]
         else:
-            M1[g] = M1[g] + R1[d]
-
-    def take1l(d):
-        g = PLACE[-d]
-        ring1[-(d + 1)].wait_recv()
-        if d == 3:
-            M1[g, 64:128] = M1[g, 64:128] + L1H[...]
+            along_zh("R", 0, part)
+            along_zh("L", 0, part)
+
+    def step_C(n):
+        if n == 1:
+            for k in range(1, 8):
+                g = PLACE[k if k <= 4 else k - 8]
+                sums["z", k] = start(remote(
+                    MC.at[g], MZ.at[k - 1], zs.at[k - 1], zr.at[k - 1], along(k)))
+        elif n == 2:
+            rows4 = MC[own]
+            for k in range(1, 8):
+                sums["z", k].wait_recv()
+                rows4 = rows4 + MZ[k - 1]
+            MX[3] = rows4
+            for k in range(3):
+                sums["x", k] = start(remote(
+                    MX.at[3], MX.at[k], xs.at[k], xr.at[k], aside(k + 1)))
         else:
-            M1[g] = M1[g] + L1[d]
-
-    def send1(d):
-        ring1[d] = start(remote(
-            M1.at[PLACE[d]], R1.at[d - 1], r1s.at[d - 1], r1r.at[d - 1], right))
-
-    def send1l(d):
-        ring1[-d] = start(remote(
-            M1.at[PLACE[-d]], L1.at[d - 1], l1s.at[d - 1], l1r.at[d - 1], left))
-
-    merge(0)
-    send0(4, 0)
-    send0l(4, 1)
-    merge(1)
-    send0(3, 1)
-    merge(2)
-    send0l(3, 0)
-    take0(3, 0)
-    send0(3, 0)
-    take0l(3, 1)
-    send0l(3, 1)
-    merge(3)
-    merge(4)
-    far1()
-    merge(5)
-    merge(6)
-    merge(7)
-    take0(2, 1)
-    send0(2, 1)
-    take0l(2, 0)
-    send0l(2, 0)
-    take0(2, 0)
-    send0(2, 0)
-    take0l(2, 1)
-    send0l(2, 1)
-    for d in (3,):
-        join(PLACE[d])
-        take1(d)
-        send1(d)
-        join(PLACE[-d])
-        take1l(d)
-        send1l(d)
-    take0(1, 1)
-    send0(1, 1)
-    take0l(1, 0)
-    send0l(1, 0)
-    take0(1, 0)
-    send0(1, 0)
-    take0l(1, 1)
-    send0l(1, 1)
-    for d in (2,):
-        join(PLACE[d])
-        take1(d)
-        send1(d)
-        join(PLACE[-d])
-        take1l(d)
-        send1l(d)
-    own = PLACE[0]
-    take0(0, 1)
-    take0l(0, 1)
-    F0[...] = M0[own, 1]
-    final = start(remote(F0, FY, fs, fr, beside))
-    for d in (1,):
-        join(PLACE[d])
-        take1(d)
-        send1(d)
-        join(PLACE[-d])
-        take1l(d)
-        send1l(d)
-    take0(0, 0)
-    take0l(0, 0)
-    join(own)
-    final.wait_recv()
-    M0[own, 0] = M0[own, 0] + FY[...]
-    MS[0] = jnp.sum(M0[own, 0].reshape(16, 8, 128), axis=0)
-    take1(0)
-    take1l(0)
-    MS[1] = jnp.sum(M1[own].reshape(16, 8, 128), axis=0)
-
-    means = [start(remote(MS, MR.at[k], ms.at[k], mr.at[k], other(k + 1)))
-             for k in range(7)]
-    for copy in means:
-        copy.wait_recv()
-    sums = MS[...]
-    for k in range(7):
-        sums = sums + MR[k]
-    mean = jnp.sum(sums, axis=1, keepdims=True) * (1.0 / 1024.0)
+            rows4 = MX[3]
+            for k in range(3):
+                sums["x", k].wait_recv()
+                rows4 = rows4 + MX[k]
+            MY[3] = rows4
+            for k in range(3):
+                sums["y", k] = start(remote(
+                    MY.at[3], MY.at[k], us.at[k], ur.at[k], over_y[k]))
+
+    MC[...] = jnp.zeros((8, 8, TBLK), F32)
+    for name in STEPS_OF_SUM:
+        kind, digits = name.rstrip("0123456789"), [int(c) for c in name if c.isdigit()]
+        if kind in ("R", "L"):
+            along_z(kind, *digits)
+        elif kind in ("Rh", "Lh"):
+            along_zh(kind[0], *digits)
+        else:
+            {"S": step_S, "M": step_M, "J": step_J, "F": step_F, "E": step_E,
+             "C": step_C}[kind](*digits)
+
+    for k in range(3):
+        sums["y", k].wait_recv()
+    mean = (MY[3, 0:2] + MY[1, 0:2] + MY[0, 2:4] + MY[2, 2:4]) * (1.0 / 1024.0)
     for h in range(2):
         block = M0[own, 0] if h == 0 else M1[own]
-        block = (block - mean[h]) * (1.0 / BLOCK)
+        block = (block - mean[h:h + 1]) * (1.0 / BLOCK)
         TMP[pl.ds(0, 64, stride=2), :] = block[0:64]
         TMP[pl.ds(1, 64, stride=2), :] = block[64:128]
         out[h * TBLK:(h + 1) * TBLK, :] = TMP[...].T
@@ -383,7 +366,7 @@
     block = (QL, TBLK)
     return pl.pallas_call(
         kernel,
-        out_shape=jax.ShapeDtypeStruct((2 * TBLK, QL), F32),
+        out_shape=pltpu.VMEM((2 * TBLK, QL), F32),
         in_specs=[pl.BlockSpec(memory_space=pl.ANY)] * 6,
         out_specs=pl.BlockSpec(memory_space=V),
         scratch_shapes=[
@@ -410,23 +393,22 @@
             V((8,) + block, F32),
             V((8,) + block, F32),
             V(block, F32),
-            V(block, F32),
-            V((7,) + block, F32),
-            V((7,) + block, F32),
-            V((64, TBLK), F32),
-            V((64, TBLK), F32),
-            V((3,) + block, F32),
-            V((3,) + block, F32),
-            V((2, 8, 128), F32),
-            V((7, 2, 8, 128), F32),
+            V((4, 4, HALF, TBLK), F32),
+            V((4, 4, HALF, TBLK), F32),
+            V((4, 2, HALF, TBLK), F32),
+            V((4, 2, HALF, TBLK), F32),
+            V((8, 8, TBLK), F32),
+            V((7, 8, TBLK), F32),
+            V((4, 8, TBLK), F32),
+            V((4, 8, TBLK), F32),
             V(block, F32),
             dma((NBUF,)), dma((NBUF,)), dma((4,)), dma,
             dma((3,)), dma((3,)), dma((7,)), dma((7,)),
-            dma((8,)), dma((8,)), dma((8,)), dma((8,)),
-            dma, dma,
-            dma((7,)), dma((7,)), dma((7,)), dma((7,)),
-            dma((4,)), dma((4,)), dma((4,)), dma((4,)),
-            dma((7,)), dma((7,)),
+            dma((8,)), dma((8,)), dma((8, 2)), dma((8, 2)),
+            dma((2,)), dma((2,)),
+            dma((4, 4)), dma((4, 4)), dma((4, 4)), dma((4, 4)),
+            dma((4, 2)), dma((4, 2)), dma((4, 2)), dma((4, 2)),
+            dma((7,)), dma((7,)), dma((3,)), dma((3,)), dma((3,)), dma((3,)),
         ],
         compiler_params=pltpu.CompilerParams(
             collective_id=0, has_side_effects=True, vmem_limit_bytes=60 * 2**20),

time: 58.7 us -> 49.9 us (0.85)
  Pallas kernels: 57 us -> 49.2 us
  local copies, waits for them, and re-layouts: 1.57 us -> 0.66 us
    pallas_call x1, Pallas kernels: 57 us -> 49.2 us  [local(): pl.pallas_call(kernel, out_shape=pltpu.VMEM((2 * TBLK, QL), F32), in_spec...]
    unnamed x1, local copies, waits for them, and re-layouts: 1.57 us -> 0.66 us
where the time goes in v3:
time: 49.9 us
  Pallas kernels  49.2 us (99%)
  local copies, waits for them, and re-layouts  0.66 us (1%)
    pallas_call x1, Pallas kernels, local(): pl.pallas_call(kernel, out_shape=pltpu.VMEM((2 * TBLK, QL), F32), in_spec...  49.2 us

profile of v3, /device:TPU:1, one launch (start us, length us, event | category | flops | bytes accessed | tf_op | source)
XLA Modules:
  0.0 49.9 jit_solution(4698888209874759086)
XLA Ops:
  0.0 49.2 %screen.1 = f32[256,128]{1,0:T(8,128)S(1)} custom-call(s32[4,64]{1,0:T(4,128)} %query_words.1, f32[64,128]{1,0:T(8,128)} %bitcast.3, s32[1,16]{1,0:T(1,128)} %bitcast.5, s32[8,16]{1,0:T(8,128)} %bitcast.4, bf16[8192,2048]{1,0:T(8,128)(2,1)} %lib.1, bf16[16,8,512,128]{3,2,1,0:T(8,128)(2,1)} %tiles.1), custom_call_target="tpu_custom_call" | custom-call | flops 8589934592 | bytes 50331648 | tf_op jit(solution)/shard_map/screen/pallas_call | solution.py:367
  49.2 0.7 %copy.8 = f32[256,128]{1,0:T(8,128)} copy(f32[256,128]{1,0:T(8,128)S(1)} %screen.1) | data formatting | bytes 262144

commit v4 on v3

--- a/solution.py
+++ b/solution.py
@@ -29,6 +29,7 @@
 ORDER = (4, 3, -3, 2, -2, 1, -1, 0)
 PLACE = {d: g for g, d in enumerate(ORDER)}
 HALF = 64
+FAR = (4, 3, 5, 2, 6, 1, 7)
 
 STEPS_OF_SUM = (
     "S0", "S1", "S2", "S3", "S4", "S5", "S6", "S7", "M0", "L42", "R41", "R40", "L43", "M1",
@@ -37,7 +38,7 @@
     "J20", "Lh30", "L22", "R21", "J21", "Lh31", "J30", "Rh30", "L23", "R20", "J31", "C2",
     "L10", "J40", "R13", "L11", "J41", "Rh21", "Lh20", "J50", "R12", "L12", "J51", "R11",
     "Lh21", "Rh20", "J60", "C3", "L13", "J61", "R10", "J70", "J71", "Rh11", "Lh10", "F2",
-    "Lh11", "Rh10", "F3", "E00", "E01", "E10", "E11",
+    "Lh11", "Rh10", "F3", "E10", "E11", "O1", "E00", "E01", "O0",
 )
 
 
@@ -53,6 +54,30 @@
     yl = p4 // 2
     core = lax.rem(p4, 2)
 
+    def square(k):
+        return (qi, z * 4 + lax.rem(p4 + k, 4))
+
+    def along(k):
+        return (qi, lax.rem(z + k + 8, 8) * 4 + p4)
+
+    def aside(k):
+        return (lax.rem(qi + 2 * k, 8), li)
+
+    high = lax.rem(qi, 2)
+    beside = (qi, z * 4 + (1 - yl) * 2 + core)
+    over_y = (beside,
+              (qi + 1 - 2 * high, li),
+              (qi + 1 - 2 * high, z * 4 + (1 - yl) * 2 + core))
+
+    group = [(qi, lax.rem(z + k, 8) * 4 + lax.rem(p4 + m, 4))
+             for k in FAR + (0,) for m in (2, 3, 1, 0) if k or m]
+    partners = list(group)
+    partners += [aside(k) for k in range(1, 4)]
+    partners += over_y[1:]
+    barrier = pltpu.get_barrier_semaphore()
+    for dev in partners:
+        pl.semaphore_signal(barrier, inc=1, device_id=dev, device_id_type=MESH)
+
     def lcp(i):
         s = lax.rem(i, NBUF)
         return pltpu.make_async_copy(
@@ -69,29 +94,6 @@
         copy.start()
     lcp(0).start()
     lcp(1).start()
-
-    def square(k):
-        return (qi, z * 4 + lax.rem(p4 + k, 4))
-
-    def along(k):
-        return (qi, lax.rem(z + k + 8, 8) * 4 + p4)
-
-    def aside(k):
-        return (lax.rem(qi + 2 * k, 8), li)
-
-    high = lax.rem(qi, 2)
-    beside = (qi, z * 4 + (1 - yl) * 2 + core)
-    over_y = (beside,
-              (qi + 1 - 2 * high, li),
-              (qi + 1 - 2 * high, z * 4 + (1 - yl) * 2 + core))
-
-    partners = [square(k) for k in (1, 2, 3)]
-    partners += [along(k) for k in range(1, 8)]
-    partners += [aside(k) for k in range(1, 4)]
-    partners += over_y[1:]
-    barrier = pltpu.get_barrier_semaphore()
-    for dev in partners:
-        pl.semaphore_signal(barrier, inc=1, device_id=dev, device_id_type=MESH)
 
     def remote(src, dst, ssem, rsem, dev):
         return pltpu.make_async_remote_copy(
@@ -146,21 +148,16 @@
         row = jnp.concatenate([W0[2 * j:2 * j + 1], W0[2 * j + 1:2 * j + 2]], axis=1)
         W[...] = jnp.where(rows == 2 * p4 + j, jnp.broadcast_to(row, (8, 128)), W[...])
     pl.semaphore_wait(barrier, len(partners))
-    one = [start(remote(W, WR.at[k], g1s.at[k], g1r.at[k], square(k + 1)))
-           for k in range(3)]
-    for copy in one:
-        copy.wait_recv()
-    W1[...] = W[...] + WR[0] + WR[1] + WR[2]
-    two = [start(remote(W1, G.at[z], g2s.at[k], g2r.at[k], along(k + 1)))
-           for k in range(7)]
-    G[z] = W1[...]
+    two = [start(remote(W, G.at[p4, z], g2s.at[k], g2r.at[k], dev))
+           for k, dev in enumerate(group)]
+    G[p4, z] = W[...]
     C[SLOTS] = jnp.zeros((QL, TBLK), F32)
     QQ[:, QL:2 * QL] = jnp.ones((NBITS, QL), F32).astype(F8)
     tabcopy.wait()
     for copy in two:
         copy.wait_recv()
 
-    turned = G[...].reshape(64, 128).T
+    turned = (G[0] + G[1] + G[2] + G[3]).reshape(64, 128).T
     panel = jnp.concatenate([turned[0:64], turned[64:128]], axis=1)
     shifts = lax.broadcasted_iota(jnp.int32, (WORDS, 32, QL), 1)
     bits = lax.shift_right_logical(
@@ -336,6 +333,17 @@
                 sums["y", k] = start(remote(
                     MY.at[3], MY.at[k], us.at[k], ur.at[k], over_y[k]))
 
+    def step_O(h):
+        if h == 1:
+            for k in range(3):
+                sums["y", k].wait_recv()
+        mean = (MY[3, h:h + 1] + MY[1, h:h + 1] + MY[0, 2 + h:3 + h]
+                + MY[2, 2 + h:3 + h]) * (1.0 / 1024.0)
+        block = ((M0[own, 0] if h == 0 else M1[own]) - mean) * (1.0 / BLOCK)
+        TMP[pl.ds(0, 64, stride=2), :] = block[0:64]
+        TMP[pl.ds(1, 64, stride=2), :] = block[64:128]
+        out[h * TBLK:(h + 1) * TBLK, :] = TMP[...].T
+
     MC[...] = jnp.zeros((8, 8, TBLK), F32)
     for name in STEPS_OF_SUM:
         kind, digits = name.rstrip("0123456789"), [int(c) for c in name if c.isdigit()]
@@ -345,17 +353,8 @@
             along_zh(kind[0], *digits)
         else:
             {"S": step_S, "M": step_M, "J": step_J, "F": step_F, "E": step_E,
-             "C": step_C}[kind](*digits)
-
-    for k in range(3):
-        sums["y", k].wait_recv()
-    mean = (MY[3, 0:2] + MY[1, 0:2] + MY[0, 2:4] + MY[2, 2:4]) * (1.0 / 1024.0)
-    for h in range(2):
-        block = M0[own, 0] if h == 0 else M1[own]
-        block = (block - mean[h:h + 1]) * (1.0 / BLOCK)
-        TMP[pl.ds(0, 64, stride=2), :] = block[0:64]
-        TMP[pl.ds(1, 64, stride=2), :] = block[64:128]
-        out[h * TBLK:(h + 1) * TBLK, :] = TMP[...].T
+             "C": step_C, "O": step_O}[kind](*digits)
+
     for copy in sent:
         copy.wait_send()
 
@@ -385,7 +384,7 @@
             V((8, 128), jnp.int32),
             V((8, 128), jnp.int32),
             V((3, 8, 128), jnp.int32),
-            V((8, 8, 128), jnp.int32),
+            V((4, 8, 8, 128), jnp.int32),
             V((8, 4) + block, F32),
             V((8, 4) + block, F32),
             V((8, 2) + block, F32),
@@ -403,7 +402,7 @@
             V((4, 8, TBLK), F32),
             V(block, F32),
             dma((NBUF,)), dma((NBUF,)), dma((4,)), dma,
-            dma((3,)), dma((3,)), dma((7,)), dma((7,)),
+            dma((3,)), dma((3,)), dma((31,)), dma((31,)),
             dma((8,)), dma((8,)), dma((8, 2)), dma((8, 2)),
             dma((2,)), dma((2,)),
             dma((4, 4)), dma((4, 4)), dma((4, 4)), dma((4, 4)),

time: 49.9 us -> 48.6 us (0.974)
  Pallas kernels: 49.2 us -> 47.8 us
    pallas_call x1, Pallas kernels: 49.2 us -> 47.8 us  [local(): pl.pallas_call(kernel, out_shape=pltpu.VMEM((2 * TBLK, QL), F32), in_spec...]
where the time goes in v4:
time: 48.6 us; the launch traced here: 48.5 us
  Pallas kernels  47.8 us (98%)
  local copies, waits for them, and re-layouts  0.66 us (1%)
    pallas_call x1, Pallas kernels, local(): pl.pallas_call(kernel, out_shape=pltpu.VMEM((2 * TBLK, QL), F32), in_spec...  47.8 us

profile of v4, /device:TPU:1, one launch (start us, length us, event | category | flops | bytes accessed | tf_op | source)
XLA Modules:
  0.0 48.5 jit_solution(34886635631889142)
XLA Ops:
  0.0 47.8 %screen.1 = f32[256,128]{1,0:T(8,128)S(1)} custom-call(s32[4,64]{1,0:T(4,128)} %query_words.1, f32[64,128]{1,0:T(8,128)} %bitcast.3, s32[1,16]{1,0:T(1,128)} %bitcast.5, s32[8,16]{1,0:T(8,128)} %bitcast.4, bf16[8192,2048]{1,0:T(8,128)(2,1)} %lib.1, bf16[16,8,512,128]{3,2,1,0:T(8,128)(2,1)} %tiles.1), custom_call_target="tpu_custom_call" | custom-call | flops 8589934592 | bytes 50331648 | tf_op jit(solution)/shard_map/screen/pallas_call | solution.py:366
  47.9 0.7 %copy.8 = f32[256,128]{1,0:T(8,128)} copy(f32[256,128]{1,0:T(8,128)S(1)} %screen.1) | data formatting | bytes 262144

commit v5 on v4

--- a/solution.py
+++ b/solution.py
@@ -196,13 +196,16 @@
     screen(0, Ss[0])
     lcp(NBUF).start()
 
-    def advance(i, u):
+    def advance(i, u, more=True):
         lcp(i + 1).wait()
         tcp(i).wait()
         hit(i, Ss[u], HTs[u])
         screen(i + 1, Ss[1 - u])
         gather_terms(i, HTs[u])
 
+        if not more:
+            return
+
         @pl.when(i + 1 + NBUF < STEPS)
         def _():
             lcp(i + 1 + NBUF).start()
@@ -217,7 +220,7 @@
         return carry
 
     lax.fori_loop(0, STEPS // 2 - 1, twice, 0)
-    advance(STEPS - 2, 0)
+    advance(STEPS - 2, 0, more=False)
     tcp(STEPS - 1).wait()
     hit(STEPS - 1, Ss[1], HTs[1])
     gather_terms(STEPS - 1, HTs[1])
@@ -342,7 +345,7 @@
         block = ((M0[own, 0] if h == 0 else M1[own]) - mean) * (1.0 / BLOCK)
         TMP[pl.ds(0, 64, stride=2), :] = block[0:64]
         TMP[pl.ds(1, 64, stride=2), :] = block[64:128]
-        out[h * TBLK:(h + 1) * TBLK, :] = TMP[...].T
+        out[h * TBLK:(h + 1) * TBLK, :] = TMP[0:QL].T
 
     MC[...] = jnp.zeros((8, 8, TBLK), F32)
     for name in STEPS_OF_SUM:
@@ -400,7 +403,7 @@
             V((7, 8, TBLK), F32),
             V((4, 8, TBLK), F32),
             V((4, 8, TBLK), F32),
-            V(block, F32),
+            V((QL + 8, TBLK), F32),
             dma((NBUF,)), dma((NBUF,)), dma((4,)), dma,
             dma((3,)), dma((3,)), dma((31,)), dma((31,)),
             dma((8,)), dma((8,)), dma((8, 2)), dma((8, 2)),

time: 48.6 us -> 48.6 us (level)
  no operation moved by 1% of the time
where the time goes in v5:
time: 48.6 us; the launch traced here: 48.5 us
  Pallas kernels  47.8 us (98%)
  local copies, waits for them, and re-layouts  0.66 us (1%)
    pallas_call x1, Pallas kernels, local(): pl.pallas_call(kernel, out_shape=pltpu.VMEM((2 * TBLK, QL), F32), in_spec...  47.8 us

profile of v5, /device:TPU:1, one launch (start us, length us, event | category | flops | bytes accessed | tf_op | source)
XLA Modules:
  0.0 48.5 jit_solution(3851154821290531953)
XLA Ops:
  0.0 47.8 %screen.1 = f32[256,128]{1,0:T(8,128)S(1)} custom-call(s32[4,64]{1,0:T(4,128)} %query_words.1, f32[64,128]{1,0:T(8,128)} %bitcast.3, s32[1,16]{1,0:T(1,128)} %bitcast.5, s32[8,16]{1,0:T(8,128)} %bitcast.4, bf16[8192,2048]{1,0:T(8,128)(2,1)} %lib.1, bf16[16,8,512,128]{3,2,1,0:T(8,128)(2,1)} %tiles.1), custom_call_target="tpu_custom_call" | custom-call | flops 8589934592 | bytes 50331648 | tf_op jit(solution)/shard_map/screen/pallas_call | solution.py:369
  47.9 0.7 %copy.8 = f32[256,128]{1,0:T(8,128)} copy(f32[256,128]{1,0:T(8,128)S(1)} %screen.1) | data formatting | bytes 262144
